TPU v7x, 32 devices: a whole 2x2x4 slice. The times are simulated.
32 devices in a mesh: row: 4 (over y, core), col: 8 (over z, x).
Axes of the slice: x: 2, y: 2, z: 4, core: 2. Of those that a mesh axis runs over, the one named last changes fastest.
Arguments:
- matrix: float32 [2048, 2048], P('row', 'col'), may hold values from -1 to 4, as said below
Outputs:
- reduced: float32 [2048, 2048], P('row', 'col')
Inputs may be any that keep to these rules, and one draw needn't show every extreme that they name: matrix is symmetric; its diagonal entries lie between 1 and 3 up to entries of size about 2048^-1/2 that every entry carries; entries at distance 256 from the diagonal with the smaller index under 2 * 256 carry an added 2.
All inputs are finite; a program needn't handle non-finite values.
Results may differ from a plain program's by a relative error of at most 0.00019.
Values sent between devices are 32-bit elements; how exact they have to be, the bound alone decides.
A program may use at most 64 MiB of HBM per device.

v0:
```python
import functools

import jax
import jax.numpy as jnp
from jax import lax
from jax.experimental import pallas as pl
from jax.experimental.pallas import tpu as pltpu
from jax.sharding import PartitionSpec as P

MESH = pl.DeviceIdType.MESH
F32 = jnp.float32


def mm(left, right, dims=((1,), (0,))):
    return lax.dot_general(
        left, right, (dims, ((), ())), precision=lax.Precision.HIGHEST, preferred_element_type=F32
    )


NT = ((1,), (1,))
TN = ((0,), (0,))


def gather_kernel(nr, nc, a_ref, pf, pi, zi, zj, gram, first, hmat, *scratch):
    (part, half_in, half_sum, half_y, red_send, red_recv, pf_send, pf_recv, ch_send, ch_recv,
     ln_send, ln_recv, top_send, top_recv) = scratch
    rows, width = a_ref.shape
    ratio = rows // width
    half = width // 2
    ny = nr // 2
    i = lax.axis_index("row")
    j = lax.axis_index("col")
    lane = lax.rem(j, ratio)
    pos = j // ratio
    core = lax.rem(i, 2)
    yy = i // 2
    base = pos * ratio

    barrier = pltpu.get_barrier_semaphore()
    for d in range(1, nr):
        pl.semaphore_signal(barrier, 1, device_id=(lax.rem(i + d, nr), j), device_id_type=MESH)
    for d in range(1, ratio):
        pl.semaphore_signal(
            barrier, 1, device_id=(i, base + lax.rem(lane + d, ratio)), device_id_type=MESH
        )

    @pl.when(pos > 0)
    def _():
        pl.semaphore_signal(barrier, 1, device_id=(i, j - ratio), device_id_type=MESH)

    @pl.when(pos < nr - 1)
    def _():
        pl.semaphore_signal(barrier, 1, device_id=(i, j + ratio), device_id_type=MESH)

    pl.semaphore_wait(
        barrier,
        nr - 1 + ratio - 1 + jnp.where(pos > 0, 1, 0) + jnp.where(pos < nr - 1, 1, 0),
    )

    def remote(src, dst, send, recv, who):
        return pltpu.make_async_remote_copy(
            src_ref=src, dst_ref=dst, send_sem=send, recv_sem=recv, device_id=who,
            device_id_type=MESH,
        )

    def column_copies(ref, sends, recvs):
        return (
            remote(ref, ref, sends.at[0], recvs, (jnp.minimum(i + 1, nr - 1), j)),
            remote(ref, ref, sends.at[1], recvs, (jnp.minimum(i + 2, nr - 1), j)),
        )

    def column_arrive(ref, sends, recvs):
        to_odd, to_even = column_copies(ref, sends, recvs)

        @pl.when(i > 0)
        def _():
            to_odd.wait_recv()

    def column_send(ref, sends, recvs):
        to_odd, to_even = column_copies(ref, sends, recvs)

        @pl.when(core == 0)
        def _():
            @pl.when(yy < ny - 1)
            def _():
                to_even.start()

            to_odd.start()

    def column_end(ref, sends, recvs):
        to_odd, to_even = column_copies(ref, sends, recvs)

        @pl.when(core == 0)
        def _():
            @pl.when(yy < ny - 1)
            def _():
                to_even.wait_send()

            to_odd.wait_send()

    def chain_copies(ref, k):
        mine = ref.at[lane]
        return (
            remote(mine, mine, ch_send.at[k, 0], ch_recv.at[k], (i, jnp.maximum(j - ratio, 0))),
            remote(mine, mine, ch_send.at[k, 1], ch_recv.at[k], (i, jnp.minimum(j + ratio, nc - 1))),
        )

    def lane_copies(ref, k):
        mine = ref.at[lane]
        out = []
        for d in range(1, ratio):
            out.append(
                remote(mine, mine, ln_send.at[k, d - 1], ln_recv.at[k, d - 1],
                       (i, base + lax.rem(lane + d, ratio)))
            )
        return out

    def chain_pass(ref, k):
        down, up = chain_copies(ref, k)

        @pl.when(pos != i)
        def _():
            down.wait_recv()

        @pl.when((pos <= i) & (pos > 0))
        def _():
            down.start()

        @pl.when((pos >= i) & (pos < nr - 1))
        def _():
            up.start()

        for c in lane_copies(ref, k):
            c.start()

    def lane_arrive(ref, k):
        for d in range(1, ratio):
            other = ref.at[lax.rem(lane - d + ratio, ratio)]
            remote(other, other, ln_send.at[k, d - 1], ln_recv.at[k, d - 1], (i, j)).wait_recv()

    def chain_end(ref, k):
        down, up = chain_copies(ref, k)

        @pl.when((pos <= i) & (pos > 0))
        def _():
            down.wait_send()

        @pl.when((pos >= i) & (pos < nr - 1))
        def _():
            up.wait_send()

        for c in lane_copies(ref, k):
            c.wait_send()

    partner = (i + 1 - 2 * core, j)
    mine_half = pl.ds(pl.multiple_of(core * half, half), half)
    other_half = pl.ds(pl.multiple_of((1 - core) * half, half), half)

    def reduce_a(k):
        return remote(part.at[k, other_half], half_in.at[k], red_send.at[k, 0], red_recv.at[k, 0], partner)

    def reduce_b(k):
        out = []
        for d in range(1, ny):
            to = lax.rem(yy + d, ny) * 2 + core
            out.append(
                remote(half_sum.at[k], half_y.at[k, yy], red_send.at[k, 1 + d],
                       red_recv.at[k, 1 + d], (to, j))
            )
        return out

    def reduce_c(k, out):
        return remote(out.at[mine_half], out.at[mine_half], red_send.at[k, 1], red_recv.at[k, 1], partner)

    def reduce_1(k):
        reduce_a(k).start()

    def reduce_2(k):
        reduce_a(k).wait_recv()
        half_sum[k] = part[k, mine_half] + half_in[k]
        for c in reduce_b(k):
            c.start()

    def reduce_3(k, out):
        for d in range(1, ny):
            slot = half_y.at[k, lax.rem(yy - d + ny, ny)]
            remote(slot, slot, red_send.at[k, 1 + d], red_recv.at[k, 1 + d], (i, j)).wait_recv()
        total = None
        for y in range(ny):
            term = jnp.where(yy == y, half_sum[k], half_y[k, y])
            total = term if total is None else total + term
        out[mine_half] = total
        reduce_c(k, out).start()

    def reduce_4(k, out):
        arrived = out.at[other_half]
        remote(arrived, arrived, red_send.at[k, 1], red_recv.at[k, 1], partner).wait_recv()

    def reduce_end(k, out):
        reduce_a(k).wait_send()
        for c in reduce_b(k):
            c.wait_send()
        reduce_c(k, out).wait_send()

    @pl.when(i == 0)
    def _():
        pf[0] = a_ref[:width] * jnp.where(j == 0, 0.0, 1.0)
        pf[1] = a_ref[width:2 * width]

    for y in range(ny):
        @pl.when(yy == y)
        def _():
            for k in range(3):
                half_y[k, y] = jnp.zeros((half, width), F32)

    for k in range(2):
        column_arrive(pf.at[k], pf_send.at[k], pf_recv.at[k])
        column_send(pf.at[k], pf_send.at[k], pf_recv.at[k])

        @pl.when(pos == i)
        def _():
            pi[k, lane] = pf[k]

        chain_pass(pi.at[k], k)

    lane_arrive(pi.at[0], 0)

    @pl.when(i == 0)
    def _():
        first[0] = pi[0, 1]
        column_send(first.at[0], top_send.at[0], top_recv.at[0])

    total = None
    for b in range(ratio):
        term = mm(pi[0, b], pi[0, b], NT)
        total = term if total is None else total + term
    part[0] = total
    reduce_1(0)
    total = None
    for b in range(ratio):
        term = mm(pi[0, b], a_ref[b * width:(b + 1) * width])
        total = term if total is None else total + term
    part[1] = total
    reduce_1(1)
    reduce_2(0)
    reduce_2(1)
    reduce_3(0, gram)
    reduce_3(1, zj)
    reduce_4(1, zj)

    @pl.when(pos == i)
    def _():
        zi[lane] = zj[...]

    chain_pass(zi, 2)
    column_arrive(first.at[0], top_send.at[0], top_recv.at[0])

    @pl.when(i > 0)
    def _():
        column_send(first.at[0], top_send.at[0], top_recv.at[0])

    lane_arrive(pi.at[1], 1)

    @pl.when(i == 0)
    def _():
        first[1] = pi[1, 1]

    column_arrive(first.at[1], top_send.at[1], top_recv.at[1])
    column_send(first.at[1], top_send.at[1], top_recv.at[1])
    lane_arrive(zi, 2)

    @pl.when(i == 0)
    def _():
        first[2] = zi[1]

    column_arrive(first.at[2], top_send.at[2], top_recv.at[2])
    column_send(first.at[2], top_send.at[2], top_recv.at[2])
    total = None
    for b in range(ratio):
        term = mm(pi[0, b], zi[b], NT)
        total = term if total is None else total + term
    part[2] = total
    reduce_1(2)
    reduce_2(2)
    reduce_3(2, hmat)
    reduce_4(2, hmat)
    reduce_4(0, gram)
    for k, out in enumerate((gram, zj, hmat)):
        reduce_end(k, out)
    for k in range(2):
        column_end(pf.at[k], pf_send.at[k], pf_recv.at[k])
        chain_end(pi.at[k], k)
    chain_end(zi, 2)
    for k in range(3):
        column_end(first.at[k], top_send.at[k], top_recv.at[k])


def small_factor(block):
    size = block.shape[0]
    step = 8
    eye = jnp.where(
        lax.broadcasted_iota(jnp.int32, (size, size), 0) == lax.broadcasted_iota(jnp.int32, (size, size), 1),
        1.0, 0.0)
    act = jnp.concatenate([block, eye], axis=1)
    lanes = 2 * size
    done = []
    for q in range(size // step):
        count = size - q * step
        rows_id = lax.broadcasted_iota(jnp.int32, (count, lanes), 0)
        cols = [
            jnp.broadcast_to(act[:, q * step + t:q * step + t + 1], (count, lanes)) for t in range(step)
        ]
        top = act[:step]
        pivots = jnp.zeros((step, lanes), F32)
        saved = []
        for t in range(step):
            pivot = cols[t][t:t + 1]
            inv = 1.0 / pivot
            mult = jnp.where(rows_id > t, cols[t], 0.0) * inv
            for u in range(t + 1, step):
                cols[u] = cols[u] - mult * cols[u][t:t + 1]
            row = top[t:t + 1]
            top = top - mult[:step] * row
            pivots = jnp.where(rows_id[:step] == t, pivot, pivots)
            saved.append((mult, row))
        done.append(top / jnp.sqrt(pivots))
        if count > step:
            rest = act[step:]
            for mult, row in saved:
                rest = rest - mult[step:] * row
            act = rest
    return jnp.concatenate(done, axis=0)[:, size:]


def update_kernel(place, a_ref, pf, pi, zi, zj, gram, first, hmat, out_ref, aug, low):
    rows, width = a_ref.shape
    ratio = rows // width
    block = 64
    i = place[0]
    j = place[1]
    one = jnp.where(
        lax.broadcasted_iota(jnp.int32, (width, width), 0)
        == lax.broadcasted_iota(jnp.int32, (width, width), 1), 1.0, 0.0)
    aug[:, :width] = gram[...]
    aug[:, width:] = one
    for q in range(width // block):
        here = slice(q * block, (q + 1) * block)
        inv = small_factor(aug[here, here])
        line = mm(inv, aug[here, :])
        low[here, :] = line[:, width:]
        if (q + 1) * block < width:
            below = slice((q + 1) * block, width)
            aug[below, :] = aug[below, :] - mm(line[:, below], line, TN)
    w = low[...]
    err = 0.5 * (one - mm(w, first[0]))

    def more(state):
        k, acc, e = state
        return (k < 40) & (jnp.max(jnp.abs(e)) > 1e-10)

    def body(state):
        k, acc, e = state
        return k + 1, acc + mm(acc, e), mm(e, e)

    _, acc, _ = lax.while_loop(more, body, (0, one + err, mm(err, err)))
    tt = 0.5 * acc
    aug[:, :width] = mm(w, first[2])
    wz = aug[:, :width]
    y = mm(mm(w, hmat[...]), w, NT) + wz + wz.T + first[1]
    half_mid = 0.5 * mm(mm(tt, y), tt, NT)

    def sides(p, f, z, is_unit):
        r = mm(w, p) + jnp.where(is_unit, one, 0.0)
        x = mm(w, z) + f
        return r, mm(tt, x) - mm(half_mid, r)

    r_cols, w_cols = sides(pf[0], pf[1], zj[...], j == 1)
    for b in range(ratio):
        r_rows, w_rows = sides(pi[0, b], pi[1, b], zi[b], i * ratio + b == 1)
        here = slice(b * width, (b + 1) * width)
        out_ref[here] = a_ref[here] - mm(w_rows, r_cols, TN) - mm(r_rows, w_cols, TN)


def solution(mesh):
    nr, nc = mesh.shape["row"], mesh.shape["col"]

    def step(matrix):
        rows, width = matrix.shape
        ratio = rows // width
        ny = nr // 2
        half = width // 2
        square = (width, width)
        vmem = pl.BlockSpec(memory_space=pltpu.VMEM)
        shapes = [(2,) + square, (2, ratio) + square, (ratio,) + square, square, square, (3,) + square, square]
        dma = pltpu.SemaphoreType.DMA
        parts = pl.pallas_call(
            functools.partial(gather_kernel, nr, nc),
            out_shape=[jax.ShapeDtypeStruct(s, F32) for s in shapes],
            in_specs=[vmem],
            out_specs=[vmem] * len(shapes),
            scratch_shapes=[
                pltpu.VMEM((3,) + square, F32),
                pltpu.VMEM((3, half, width), F32),
                pltpu.VMEM((3, half, width), F32),
                pltpu.VMEM((3, ny, half, width), F32),
                dma((3, ny + 1)), dma((3, ny + 1)),
                dma((2, 2)), dma((2,)),
                dma((3, 2)), dma((3,)),
                dma((3, ratio - 1)), dma((3, ratio - 1)),
                dma((3, 2)), dma((3,)),
            ],
            compiler_params=pltpu.CompilerParams(
                collective_id=0, has_side_effects=True, vmem_limit_bytes=48 * 2**20
            ),
            name="gather",
        )(matrix)
        return pl.pallas_call(
            update_kernel,
            out_shape=jax.ShapeDtypeStruct(matrix.shape, F32),
            in_specs=[pl.BlockSpec(memory_space=pltpu.SMEM)] + [vmem] * 8,
            out_specs=vmem,
            scratch_shapes=[pltpu.VMEM((width, 2 * width), F32), pltpu.VMEM(square, F32)],
            compiler_params=pltpu.CompilerParams(vmem_limit_bytes=48 * 2**20),
            name="update",
        )(jnp.stack([lax.axis_index("row"), lax.axis_index("col")]), matrix, *parts)

    return jax.shard_map(
        step, mesh=mesh, in_specs=(P("row", "col"),), out_specs=P("row", "col"), check_vma=False
    )
```

profile of v0, /device:TPU:25, one launch (start us, length us, event | category | flops | bytes accessed | tf_op | source)
XLA Modules:
  0.0 108.7 jit_solution(8320885767232101583)
XLA Ops:
  0.0 0.1 pad_add_fusion.place
  0.1 0.0 copy-start
  0.1 1.0 copy-done
  1.1 86.9 %gather.1 = (f32[2,256,256]{2,1,0:T(8,128)S(1)}, f32[2,2,256,256]{3,2,1,0:T(8,128)S(1)}, f32[2,256,256]{2,1,0:T(8,128)S(1)}, f32[256,256]{1,0:T(8,128)S(1)}, f32...) custom-call(f32[512,256]{1,0:T(8,128)S(1)} %copy-done), custom_call_target="tpu_custom_call" | custom-call | tf_op jit(solution)/shard_map/gather/pallas_call | solution.py:396
  88.0 20.6 %update.1 = f32[512,256]{1,0:T(8,128)} custom-call(s32[2]{0:T(128)S(1)} %pad_add_fusion.place, f32[512,256]{1,0:T(8,128)S(1)} %copy-done, f32[2,256,256]{2,1,0:T(8,128)S(1)} %get-tuple-element.12.pf, f32[2,2,256,256]{3,2,1,0:T(8,128)S(1)} %get-tuple-element.13.pi, f32[2,256,256]{2,1,0:T(8,128)S(1)} %get-tuple-element.14.zi, ...), custom_call_target="tpu_custom_call" | custom-call | tf_op jit(solution)/shard_map/update/pallas_call | solution.py:417
Async XLA Ops:
  0.1 1.0 copy-start
where the time goes:
time: 109 us
  Pallas kernels  108 us (99%)
    pallas_call x1, Pallas kernels, step(): pl.pallas_call(functools.partial(gather_kernel, nr, nc), out_shape=[jax.S...  86.9 us
    pallas_call x1, Pallas kernels, step(): pl.pallas_call(update_kernel, out_shape=jax.ShapeDtypeStruct(matrix.shape...  20.6 us

commit v1 on v0

v1 whole, which is shorter than its diff:
```python
import functools

import jax
import jax.numpy as jnp
from jax import lax
from jax.experimental import pallas as pl
from jax.experimental.pallas import tpu as pltpu
from jax.sharding import PartitionSpec as P

MESH = pl.DeviceIdType.MESH
F32 = jnp.float32
CHUNKS = 4
BLOCK = 64


def mm(left, right, dims=((1,), (0,))):
    return lax.dot_general(
        left, right, (dims, ((), ())), precision=lax.Precision.HIGHEST, preferred_element_type=F32
    )


NT = ((1,), (1,))
TN = ((0,), (0,))


def unit(size):
    same = lax.broadcasted_iota(jnp.int32, (size, size), 0) == lax.broadcasted_iota(jnp.int32, (size, size), 1)
    return jnp.where(same, 1.0, 0.0)


def gather_kernel(nr, nc, a_ref, pf, zj, low, first, ri, xi, ymat, *scratch):
    (pi, zi, gram, aug, part, half_in, half_sum, half_y, red_send, red_recv, pf_send, pf_recv, ch_send, ch_recv,
     ln_send, ln_recv, top_send, top_recv) = scratch
    rows, width = a_ref.shape
    ratio = rows // width
    half = width // 2
    ny = nr // 2
    i = lax.axis_index("row")
    j = lax.axis_index("col")
    lane = lax.rem(j, ratio)
    pos = j // ratio
    core = lax.rem(i, 2)
    yy = i // 2
    base = pos * ratio

    barrier = pltpu.get_barrier_semaphore()
    for d in range(1, nr):
        pl.semaphore_signal(barrier, 1, device_id=(lax.rem(i + d, nr), j), device_id_type=MESH)
    for d in range(1, ratio):
        pl.semaphore_signal(
            barrier, 1, device_id=(i, base + lax.rem(lane + d, ratio)), device_id_type=MESH
        )

    @pl.when(pos > 0)
    def _():
        pl.semaphore_signal(barrier, 1, device_id=(i, j - ratio), device_id_type=MESH)

    @pl.when(pos < nr - 1)
    def _():
        pl.semaphore_signal(barrier, 1, device_id=(i, j + ratio), device_id_type=MESH)

    pl.semaphore_wait(
        barrier,
        nr - 1 + ratio - 1 + jnp.where(pos > 0, 1, 0) + jnp.where(pos < nr - 1, 1, 0),
    )

    def remote(src, dst, send, recv, who):
        return pltpu.make_async_remote_copy(
            src_ref=src, dst_ref=dst, send_sem=send, recv_sem=recv, device_id=who,
            device_id_type=MESH,
        )

    chunk = width // CHUNKS
    spans = [pl.ds(c * chunk, chunk) for c in range(CHUNKS)]
    away = jnp.abs(pos - i)

    def column_copies(ref, sends, recv):
        return (
            remote(ref, ref, sends.at[0], recv, (jnp.minimum(i + 1, nr - 1), j)),
            remote(ref, ref, sends.at[1], recv, (jnp.minimum(i + 2, nr - 1), j)),
        )

    def column_arrive(ref, sends, recv):
        @pl.when(i > 0)
        def _():
            column_copies(ref, sends, recv)[0].wait_recv()

    def column_send(ref, sends, recv):
        @pl.when(core == 0)
        def _():
            to_odd, to_even = column_copies(ref, sends, recv)

            @pl.when(yy < ny - 1)
            def _():
                to_even.start()

            to_odd.start()

    def column_end(ref, sends, recv):
        @pl.when(core == 0)
        def _():
            to_odd, to_even = column_copies(ref, sends, recv)

            @pl.when(yy < ny - 1)
            def _():
                to_even.wait_send()

            to_odd.wait_send()

    def chain_copies(ref, k, c):
        mine = ref.at[lane, spans[c]]
        return (
            remote(mine, mine, ch_send.at[k, c, 0], ch_recv.at[k, c], (i, jnp.maximum(j - ratio, 0))),
            remote(mine, mine, ch_send.at[k, c, 1], ch_recv.at[k, c], (i, jnp.minimum(j + ratio, nc - 1))),
        )

    def lane_copies(ref, k, c):
        mine = ref.at[lane, spans[c]]
        return [
            remote(mine, mine, ln_send.at[k, c, d - 1], ln_recv.at[k, c, d - 1],
                   (i, base + lax.rem(lane + d, ratio)))
            for d in range(1, ratio)
        ]

    def chain_push(ref, k, c):
        down, up = chain_copies(ref, k, c)

        @pl.when((pos <= i) & (pos > 0))
        def _():
            down.start()

        @pl.when((pos >= i) & (pos < nr - 1))
        def _():
            up.start()

        for copy in lane_copies(ref, k, c):
            copy.start()

    def chain_source(ref, k, c, block):
        @pl.when(away == 0)
        def _():
            ref[lane, spans[c]] = block[spans[c]]
            chain_push(ref, k, c)

    def chain_pass(ref, k, c, far):
        @pl.when(far)
        def _():
            chain_copies(ref, k, c)[0].wait_recv()
            chain_push(ref, k, c)

    def chain_point(ref, k, point):
        for c in range(CHUNKS):
            distance = point - c // 2
            if 1 <= distance < nr:
                chain_pass(ref, k, c, away == distance)

    def lane_arrive(ref, k):
        for c in range(CHUNKS):
            for d in range(1, ratio):
                other = ref.at[lax.rem(lane - d + ratio, ratio), spans[c]]
                remote(other, other, ln_send.at[k, c, d - 1], ln_recv.at[k, c, d - 1], (i, j)).wait_recv()

    def chain_end(ref, k):
        for c in range(CHUNKS):
            down, up = chain_copies(ref, k, c)

            @pl.when((pos <= i) & (pos > 0))
            def _():
                down.wait_send()

            @pl.when((pos >= i) & (pos < nr - 1))
            def _():
                up.wait_send()

            for copy in lane_copies(ref, k, c):
                copy.wait_send()

    partner = (i + 1 - 2 * core, j)
    mine_half = pl.ds(pl.multiple_of(core * half, half), half)
    other_half = pl.ds(pl.multiple_of((1 - core) * half, half), half)

    def reduce_a(k):
        return remote(part.at[k, other_half], half_in.at[k], red_send.at[k, 0], red_recv.at[k, 0], partner)

    def reduce_b(k):
        out = []
        for d in range(1, ny):
            to = lax.rem(yy + d, ny) * 2 + core
            out.append(
                remote(half_sum.at[k], half_y.at[k, yy], red_send.at[k, 1 + d],
                       red_recv.at[k, 1 + d], (to, j))
            )
        return out

    def reduce_c(k, out):
        return remote(out.at[mine_half], out.at[mine_half], red_send.at[k, 1], red_recv.at[k, 1], partner)

    def reduce_1(k):
        reduce_a(k).start()

    def reduce_2(k):
        reduce_a(k).wait_recv()
        half_sum[k] = part[k, mine_half] + half_in[k]
        for c in reduce_b(k):
            c.start()

    def reduce_3(k, out):
        for d in range(1, ny):
            slot = half_y.at[k, lax.rem(yy - d + ny, ny)]
            remote(slot, slot, red_send.at[k, 1 + d], red_recv.at[k, 1 + d], (i, j)).wait_recv()
        total = None
        for y in range(ny):
            term = jnp.where(yy == y, half_sum[k], half_y[k, y])
            total = term if total is None else total + term
        out[mine_half] = total
        reduce_c(k, out).start()

    def reduce_4(k, out):
        arrived = out.at[other_half]
        remote(arrived, arrived, red_send.at[k, 1], red_recv.at[k, 1], partner).wait_recv()

    def reduce_end(k, out):
        reduce_a(k).wait_send()
        for c in reduce_b(k):
            c.wait_send()
        reduce_c(k, out).wait_send()

    for y in range(ny):
        @pl.when(yy == y)
        def _():
            for k in range(3):
                half_y[k, y] = jnp.zeros((half, width), F32)

    @pl.when(i == 0)
    def _():
        pf[0] = a_ref[:width] * jnp.where(j == 0, 0.0, 1.0)
        pf[1] = a_ref[width:2 * width]

    def column_step(k, c):
        block = pf.at[k, spans[c]]
        column_arrive(block, pf_send.at[k, c], pf_recv.at[k, c])
        column_send(block, pf_send.at[k, c], pf_recv.at[k, c])

    p_rows, f_rows = pi.at[0], pi.at[1]
    for c in range(CHUNKS + 1):
        if c < CHUNKS:
            column_step(0, c)
            chain_source(p_rows, 0, c, pf.at[0])
        if c >= 1:
            chain_pass(p_rows, 0, c - 1, away > 0)
    for c in range(CHUNKS):
        column_step(1, c)
    lane_arrive(p_rows, 0)

    total = None
    for b in range(ratio):
        term = mm(pi[0, b], pi[0, b], NT)
        total = term if total is None else total + term
    part[0] = total
    reduce_1(0)
    total = None
    for b in range(ratio):
        term = mm(pi[0, b], a_ref[b * width:(b + 1) * width])
        total = term if total is None else total + term
    part[1] = total
    reduce_1(1)
    for c in range(CHUNKS):
        chain_source(f_rows, 1, c, pf.at[1])
    reduce_2(0)
    reduce_2(1)
    reduce_3(0, gram)
    reduce_3(1, zj)
    reduce_4(1, zj)
    for c in range(CHUNKS):
        chain_source(zi, 2, c, zj)

    @pl.when(i == 0)
    def _():
        first[...] = pi[0, 1]
        column_send(first, top_send, top_recv.at[0])

    chain_point(f_rows, 1, 1)
    chain_point(f_rows, 1, 2)
    reduce_4(0, gram)

    one = unit(width)
    aug[:, :width] = gram[...]
    aug[:, width:] = one
    steps = width // BLOCK
    last = nr - 1 + (CHUNKS - 1) // 2
    for q in range(steps):
        here = slice(q * BLOCK, (q + 1) * BLOCK)
        line = mm(small_factor(aug[here, here]), aug[here, :])
        low[here, :] = line[:, width:]
        if q + 1 < steps:
            below = slice((q + 1) * BLOCK, width)
            aug[below, :] = aug[below, :] - mm(line[:, below], line, TN)
        if q + 3 <= last:
            chain_point(f_rows, 1, q + 3)
        if q + 1 <= last:
            chain_point(zi, 2, q + 1)
    for point in range(steps + 1, last + 1):
        if point + 2 <= last:
            chain_point(f_rows, 1, point + 2)
        chain_point(zi, 2, point)

    column_arrive(first, top_send, top_recv.at[0])

    @pl.when(i > 0)
    def _():
        column_send(first, top_send, top_recv.at[0])

    for b in range(ratio):
        ri[b] = mm(low[...], pi[0, b]) + one * jnp.where(i * ratio + b == 1, 1.0, 0.0)
    lane_arrive(f_rows, 1)
    lane_arrive(zi, 2)
    total = None
    for b in range(ratio):
        xi[b] = mm(low[...], zi[b]) + pi[1, b]
        term = mm(ri[b], xi[b], NT)
        total = term if total is None else total + term
    part[2] = total
    reduce_1(2)
    reduce_2(2)
    reduce_3(2, ymat)
    reduce_4(2, ymat)
    for k, out in enumerate((gram, zj, ymat)):
        reduce_end(k, out)
    for k in range(2):
        for c in range(CHUNKS):
            column_end(pf.at[k, spans[c]], pf_send.at[k, c], pf_recv.at[k, c])
    for k, ref in enumerate((p_rows, f_rows, zi)):
        chain_end(ref, k)
    column_end(first, top_send, top_recv.at[0])


def small_factor(block):
    size = block.shape[0]
    step = 8
    eye = unit(size)
    act = jnp.concatenate([block, eye], axis=1)
    lanes = 2 * size
    done = []
    for q in range(size // step):
        count = size - q * step
        rows_id = lax.broadcasted_iota(jnp.int32, (count, lanes), 0)
        cols = [
            jnp.broadcast_to(act[:, q * step + t:q * step + t + 1], (count, lanes)) for t in range(step)
        ]
        top = act[:step]
        pivots = jnp.zeros((step, lanes), F32)
        saved = []
        for t in range(step):
            pivot = cols[t][t:t + 1]
            inv = 1.0 / pivot
            mult = jnp.where(rows_id > t, cols[t], 0.0) * inv
            for u in range(t + 1, step):
                cols[u] = cols[u] - mult * cols[u][t:t + 1]
            row = top[t:t + 1]
            top = top - mult[:step] * row
            pivots = jnp.where(rows_id[:step] == t, pivot, pivots)
            saved.append((mult, row))
        done.append(top / jnp.sqrt(pivots))
        if count > step:
            rest = act[step:]
            for mult, row in saved:
                rest = rest - mult[step:] * row
            act = rest
    return jnp.concatenate(done, axis=0)[:, size:]


def update_kernel(place, a_ref, pf, zj, low, first, ri, xi, ymat, out_ref, tt_ref, mid_ref):
    rows, width = a_ref.shape
    ratio = rows // width
    j = place[0]
    one = unit(width)
    w = low[...]
    err = 0.5 * (one - mm(w, first[...]))

    def more(state):
        k, acc, e = state
        return (k < 40) & (jnp.max(jnp.abs(e)) > 1e-10)

    def body(state):
        k, acc, e = state
        return k + 1, acc + mm(acc, e), mm(e, e)

    _, acc, _ = lax.while_loop(more, body, (0, one + err, mm(err, err)))
    tt_ref[...] = 0.5 * acc
    mid_ref[...] = mm(tt_ref[...], ymat[...])
    mid_ref[...] = 0.5 * mm(mid_ref[...], tt_ref[...], NT)

    def sides(r, x):
        return mm(tt_ref[...], x) - mm(mid_ref[...], r)

    r_cols = mm(w, pf[0]) + one * jnp.where(j == 1, 1.0, 0.0)
    w_cols = sides(r_cols, mm(w, zj[...]) + pf[1])
    for b in range(ratio):
        w_rows = sides(ri[b], xi[b])
        here = slice(b * width, (b + 1) * width)
        out_ref[here] = a_ref[here] - mm(w_rows, r_cols, TN) - mm(ri[b], w_cols, TN)


def solution(mesh):
    nr, nc = mesh.shape["row"], mesh.shape["col"]

    def step(matrix):
        rows, width = matrix.shape
        ratio = rows // width
        ny = nr // 2
        half = width // 2
        square = (width, width)
        vmem = pl.BlockSpec(memory_space=pltpu.VMEM)
        blocks = (ratio,) + square
        shapes = [(2,) + square, square, square, square, blocks, blocks, square]
        dma = pltpu.SemaphoreType.DMA
        parts = pl.pallas_call(
            functools.partial(gather_kernel, nr, nc),
            out_shape=[jax.ShapeDtypeStruct(s, F32) for s in shapes],
            in_specs=[vmem],
            out_specs=[vmem] * len(shapes),
            scratch_shapes=[
                pltpu.VMEM((2,) + blocks, F32),
                pltpu.VMEM(blocks, F32),
                pltpu.VMEM(square, F32),
                pltpu.VMEM((width, 2 * width), F32),
                pltpu.VMEM((3,) + square, F32),
                pltpu.VMEM((3, half, width), F32),
                pltpu.VMEM((3, half, width), F32),
                pltpu.VMEM((3, ny, half, width), F32),
                dma((3, ny + 1)), dma((3, ny + 1)),
                dma((2, CHUNKS, 2)), dma((2, CHUNKS)),
                dma((3, CHUNKS, 2)), dma((3, CHUNKS)),
                dma((3, CHUNKS, ratio - 1)), dma((3, CHUNKS, ratio - 1)),
                dma((2,)), dma((1,)),
            ],
            compiler_params=pltpu.CompilerParams(
                collective_id=0, has_side_effects=True, vmem_limit_bytes=48 * 2**20
            ),
            name="gather",
        )(matrix)
        return pl.pallas_call(
            update_kernel,
            out_shape=jax.ShapeDtypeStruct(matrix.shape, F32),
            in_specs=[pl.BlockSpec(memory_space=pltpu.SMEM)] + [vmem] * 8,
            out_specs=vmem,
            scratch_shapes=[pltpu.VMEM(square, F32), pltpu.VMEM(square, F32)],
            compiler_params=pltpu.CompilerParams(vmem_limit_bytes=48 * 2**20),
            name="update",
        )(lax.axis_index("col").reshape(1), matrix, *parts)

    return jax.shard_map(
        step, mesh=mesh, in_specs=(P("row", "col"),), out_specs=P("row", "col"), check_vma=False
    )
```

time: 109 us -> 73.7 us (0.68)
  the two profiles are of different devices: /device:TPU:25 before, /device:TPU:31 now
where the time goes in v1:
time: 73.7 us; the launch traced here: 73.5 us
  Pallas kernels  72.5 us (98%)
  local copies, waits for them, and re-layouts  1.04 us (1%)
    pallas_call x1, Pallas kernels, step(): pl.pallas_call(functools.partial(gather_kernel, nr, nc), out_shape=[jax.S...  64 us
    pallas_call x1, Pallas kernels, step(): pl.pallas_call(update_kernel, out_shape=jax.ShapeDtypeStruct(matrix.shape...  8.51 us

profile of v1, /device:TPU:31, one launch (start us, length us, event | category | flops | bytes accessed | tf_op | source)
XLA Modules:
  0.0 73.5 jit_solution(13544063161476245627)
XLA Ops:
  0.0 0.0 copy-start
  0.0 1.0 %copy-done = f32[512,256]{1,0:T(8,128)S(1)} copy-done((f32[512,256]{1,0:T(8,128)S(1)}, f32[512,256]{1,0:T(8,128)}, u32[]{:S(2)}) %copy-start) | copy-done | bytes 524312
  1.0 64.0 %gather.1 = (f32[2,256,256]{2,1,0:T(8,128)S(1)}, f32[256,256]{1,0:T(8,128)S(1)}, f32[256,256]{1,0:T(8,128)S(1)}, f32[256,256]{1,0:T(8,128)S(1)}, f32[2,256,256]{...) custom-call(f32[512,256]{1,0:T(8,128)S(1)} %copy-done), custom_call_target="tpu_custom_call" | custom-call | tf_op jit(solution)/shard_map/gather/pallas_call | solution.py:417
  65.0 8.5 %update.1 = f32[512,256]{1,0:T(8,128)} custom-call(s32[1]{0:T(128)} %bitcast.place, f32[512,256]{1,0:T(8,128)S(1)} %copy-done, f32[2,256,256]{2,1,0:T(8,128)S(1)} %get-tuple-element.12.pf, f32[256,256]{1,0:T(8,128)S(1)} %get-tuple-element.13.zj, f32[256,256]{1,0:T(8,128)S(1)} %get-tuple-element.14.low, f32[256,256]{1,0:T(8,128)S(1)} %get-tuple-element.15.first, ...), custom_call_target="tpu_custom_call" | custom-call | tf_op jit(solution)/shard_map/update/pallas_call | solution.py:442
Async XLA Ops:
  0.0 1.0 %copy-start = (f32[512,256]{1,0:T(8,128)S(1)}, f32[512,256]{1,0:T(8,128)}, u32[]{:S(2)}) copy-start(f32[512,256]{1,0:T(8,128)} %a_ref.3) | copy-start | bytes 1572868

commit v2 on v1

--- a/solution.py
+++ b/solution.py
@@ -9,7 +9,7 @@
 
 MESH = pl.DeviceIdType.MESH
 F32 = jnp.float32
-CHUNKS = 4
+CHUNKS = 8
 BLOCK = 64
 
 
@@ -19,6 +19,21 @@
     )
 
 
+def halves(x):
+    high = x.astype(jnp.bfloat16)
+    return high, (x - high.astype(F32)).astype(jnp.bfloat16)
+
+
+def mm3(left, right, dims=((1,), (0,))):
+    lh, ll = halves(left)
+    rh, rl = halves(right)
+
+    def dot(a, b):
+        return lax.dot_general(a, b, (dims, ((), ())), preferred_element_type=F32)
+
+    return dot(lh, rl) + dot(ll, rh) + dot(lh, rh)
+
+
 NT = ((1,), (1,))
 TN = ((0,), (0,))
 
@@ -28,8 +43,14 @@
     return jnp.where(same, 1.0, 0.0)
 
 
-def gather_kernel(nr, nc, a_ref, pf, zj, low, first, ri, xi, ymat, *scratch):
-    (pi, zi, gram, aug, part, half_in, half_sum, half_y, red_send, red_recv, pf_send, pf_recv, ch_send, ch_recv,
+def doubling(acc, rest):
+    e = rest[...]
+    acc[...] = acc[...] + mm3(acc[...], e)
+    rest[...] = mm3(e, e)
+
+
+def gather_kernel(nr, nc, a_ref, acc, rest, rj, xj, ri, xi, ymat, *scratch):
+    (pf, zj, low, first, pi, zi, gram, aug, part, half_in, half_sum, half_y, red_send, red_recv, pf_send, pf_recv, ch_send, ch_recv,
      ln_send, ln_recv, top_send, top_recv) = scratch
     rows, width = a_ref.shape
     ratio = rows // width
@@ -150,7 +171,7 @@
 
     def chain_point(ref, k, point):
         for c in range(CHUNKS):
-            distance = point - c // 2
+            distance = point - 2 * c // CHUNKS
             if 1 <= distance < nr:
                 chain_pass(ref, k, c, away == distance)
 
@@ -254,13 +275,13 @@
 
     total = None
     for b in range(ratio):
-        term = mm(pi[0, b], pi[0, b], NT)
+        term = mm3(pi[0, b], pi[0, b], NT)
         total = term if total is None else total + term
     part[0] = total
     reduce_1(0)
     total = None
     for b in range(ratio):
-        term = mm(pi[0, b], a_ref[b * width:(b + 1) * width])
+        term = mm3(pi[0, b], a_ref[b * width:(b + 1) * width])
         total = term if total is None else total + term
     part[1] = total
     reduce_1(1)
@@ -279,15 +300,14 @@
         first[...] = pi[0, 1]
         column_send(first, top_send, top_recv.at[0])
 
+    reduce_4(0, gram)
     chain_point(f_rows, 1, 1)
-    chain_point(f_rows, 1, 2)
-    reduce_4(0, gram)
 
     one = unit(width)
     aug[:, :width] = gram[...]
     aug[:, width:] = one
     steps = width // BLOCK
-    last = nr - 1 + (CHUNKS - 1) // 2
+    last = nr
     for q in range(steps):
         here = slice(q * BLOCK, (q + 1) * BLOCK)
         line = mm(small_factor(aug[here, here]), aug[here, :])
@@ -295,13 +315,13 @@
         if q + 1 < steps:
             below = slice((q + 1) * BLOCK, width)
             aug[below, :] = aug[below, :] - mm(line[:, below], line, TN)
-        if q + 3 <= last:
-            chain_point(f_rows, 1, q + 3)
+        if q + 2 <= last:
+            chain_point(f_rows, 1, q + 2)
         if q + 1 <= last:
             chain_point(zi, 2, q + 1)
     for point in range(steps + 1, last + 1):
-        if point + 2 <= last:
-            chain_point(f_rows, 1, point + 2)
+        if point + 1 <= last:
+            chain_point(f_rows, 1, point + 1)
         chain_point(zi, 2, point)
 
     column_arrive(first, top_send, top_recv.at[0])
@@ -311,18 +331,27 @@
         column_send(first, top_send, top_recv.at[0])
 
     for b in range(ratio):
-        ri[b] = mm(low[...], pi[0, b]) + one * jnp.where(i * ratio + b == 1, 1.0, 0.0)
+        ri[b] = mm3(low[...], pi[0, b]) + one * jnp.where(i * ratio + b == 1, 1.0, 0.0)
     lane_arrive(f_rows, 1)
     lane_arrive(zi, 2)
     total = None
     for b in range(ratio):
-        xi[b] = mm(low[...], zi[b]) + pi[1, b]
-        term = mm(ri[b], xi[b], NT)
+        xi[b] = mm3(low[...], zi[b]) + pi[1, b]
+        term = mm3(ri[b], xi[b], NT)
         total = term if total is None else total + term
     part[2] = total
     reduce_1(2)
+    err = 0.5 * (one - mm3(low[...], first[...]))
+    acc[...] = one + err
+    rest[...] = mm3(err, err)
+    doubling(acc, rest)
     reduce_2(2)
+    doubling(acc, rest)
+    doubling(acc, rest)
+    rj[...] = mm3(low[...], pf[0]) + one * jnp.where(j == 1, 1.0, 0.0)
+    xj[...] = mm3(low[...], zj[...]) + pf[1]
     reduce_3(2, ymat)
+    doubling(acc, rest)
     reduce_4(2, ymat)
     for k, out in enumerate((gram, zj, ymat)):
         reduce_end(k, out)
@@ -369,36 +398,33 @@
     return jnp.concatenate(done, axis=0)[:, size:]
 
 
-def update_kernel(place, a_ref, pf, zj, low, first, ri, xi, ymat, out_ref, tt_ref, mid_ref):
+def update_kernel(a_ref, acc, rest, rj, xj, ri, xi, ymat, out_ref, tt_ref, mid_ref, rest_ref):
     rows, width = a_ref.shape
     ratio = rows // width
-    j = place[0]
-    one = unit(width)
-    w = low[...]
-    err = 0.5 * (one - mm(w, first[...]))
+    tt_ref[...] = acc[...]
+    rest_ref[...] = rest[...]
 
     def more(state):
-        k, acc, e = state
-        return (k < 40) & (jnp.max(jnp.abs(e)) > 1e-10)
+        k, size = state
+        return (k < 40) & (size > 1e-10)
 
     def body(state):
-        k, acc, e = state
-        return k + 1, acc + mm(acc, e), mm(e, e)
-
-    _, acc, _ = lax.while_loop(more, body, (0, one + err, mm(err, err)))
-    tt_ref[...] = 0.5 * acc
-    mid_ref[...] = mm(tt_ref[...], ymat[...])
-    mid_ref[...] = 0.5 * mm(mid_ref[...], tt_ref[...], NT)
+        doubling(tt_ref, rest_ref)
+        return state[0] + 1, jnp.max(jnp.abs(rest_ref[...]))
+
+    lax.while_loop(more, body, (0, jnp.max(jnp.abs(rest_ref[...]))))
+    tt_ref[...] = 0.5 * tt_ref[...]
+    mid_ref[...] = mm3(tt_ref[...], ymat[...])
+    mid_ref[...] = 0.5 * mm3(mid_ref[...], tt_ref[...], NT)
 
     def sides(r, x):
-        return mm(tt_ref[...], x) - mm(mid_ref[...], r)
-
-    r_cols = mm(w, pf[0]) + one * jnp.where(j == 1, 1.0, 0.0)
-    w_cols = sides(r_cols, mm(w, zj[...]) + pf[1])
+        return mm3(tt_ref[...], x) - mm3(mid_ref[...], r)
+
+    w_cols = sides(rj[...], xj[...])
     for b in range(ratio):
         w_rows = sides(ri[b], xi[b])
         here = slice(b * width, (b + 1) * width)
-        out_ref[here] = a_ref[here] - mm(w_rows, r_cols, TN) - mm(ri[b], w_cols, TN)
+        out_ref[here] = a_ref[here] - mm3(w_rows, rj[...], TN) - mm3(ri[b], w_cols, TN)
 
 
 def solution(mesh):
@@ -412,7 +438,7 @@
         square = (width, width)
         vmem = pl.BlockSpec(memory_space=pltpu.VMEM)
         blocks = (ratio,) + square
-        shapes = [(2,) + square, square, square, square, blocks, blocks, square]
+        shapes = [square, square, square, square, blocks, blocks, square]
         dma = pltpu.SemaphoreType.DMA
         parts = pl.pallas_call(
             functools.partial(gather_kernel, nr, nc),
@@ -420,6 +446,10 @@
             in_specs=[vmem],
             out_specs=[vmem] * len(shapes),
             scratch_shapes=[
+                pltpu.VMEM((2,) + square, F32),
+                pltpu.VMEM(square, F32),
+                pltpu.VMEM(square, F32),
+                pltpu.VMEM(square, F32),
                 pltpu.VMEM((2,) + blocks, F32),
                 pltpu.VMEM(blocks, F32),
                 pltpu.VMEM(square, F32),
@@ -442,12 +472,12 @@
         return pl.pallas_call(
             update_kernel,
             out_shape=jax.ShapeDtypeStruct(matrix.shape, F32),
-            in_specs=[pl.BlockSpec(memory_space=pltpu.SMEM)] + [vmem] * 8,
+            in_specs=[vmem] * 8,
             out_specs=vmem,
-            scratch_shapes=[pltpu.VMEM(square, F32), pltpu.VMEM(square, F32)],
+            scratch_shapes=[pltpu.VMEM(square, F32)] * 3,
             compiler_params=pltpu.CompilerParams(vmem_limit_bytes=48 * 2**20),
             name="update",
-        )(lax.axis_index("col").reshape(1), matrix, *parts)
+        )(matrix, *parts)
 
     return jax.shard_map(
         step, mesh=mesh, in_specs=(P("row", "col"),), out_specs=P("row", "col"), check_vma=False

time: 73.7 us -> 66.6 us (0.904)
  Pallas kernels: 72.5 us -> 65.1 us
    pallas_call x1, Pallas kernels: 8.51 us -> 3.02 us  [step(): pl.pallas_call(update_kernel, out_shape=jax.ShapeDtypeStruct(matrix.shape...]
    pallas_call x1, Pallas kernels: 64 us -> 62.1 us  [step(): pl.pallas_call(functools.partial(gather_kernel, nr, nc), out_shape=[jax.S...]
where the time goes in v2:
time: 66.6 us; the launch traced here: 66.2 us
  Pallas kernels  65.1 us (98%)
  local copies, waits for them, and re-layouts  1.04 us (2%)
    pallas_call x1, Pallas kernels, step(): pl.pallas_call(functools.partial(gather_kernel, nr, nc), out_shape=[jax.S...  62.1 us
    pallas_call x1, Pallas kernels, step(): pl.pallas_call(update_kernel, out_shape=jax.ShapeDtypeStruct(matrix.shape...  3.02 us

profile of v2, /device:TPU:31, one launch (start us, length us, event | category | flops | bytes accessed | tf_op | source)
XLA Modules:
  0.0 66.2 jit_solution(9913481347339864749)
XLA Ops:
  0.0 0.0 copy-start
  0.0 1.0 %copy-done = f32[512,256]{1,0:T(8,128)S(1)} copy-done((f32[512,256]{1,0:T(8,128)S(1)}, f32[512,256]{1,0:T(8,128)}, u32[]{:S(2)}) %copy-start) | copy-done | bytes 524312
  1.0 62.1 %gather.1 = (f32[256,256]{1,0:T(8,128)S(1)}, f32[256,256]{1,0:T(8,128)S(1)}, f32[256,256]{1,0:T(8,128)S(1)}, f32[256,256]{1,0:T(8,128)S(1)}, f32[2,256,256]{2,1,...) custom-call(f32[512,256]{1,0:T(8,128)S(1)} %copy-done), custom_call_target="tpu_custom_call" | custom-call | tf_op jit(solution)/shard_map/gather/pallas_call | solution.py:443
  63.1 3.0 %update.1 = f32[512,256]{1,0:T(8,128)} custom-call(f32[512,256]{1,0:T(8,128)S(1)} %copy-done, f32[256,256]{1,0:T(8,128)S(1)} %get-tuple-element.12.acc, f32[256,256]{1,0:T(8,128)S(1)} %get-tuple-element.13.rest, f32[256,256]{1,0:T(8,128)S(1)} %get-tuple-element.14.rj, f32[256,256]{1,0:T(8,128)S(1)} %get-tuple-element.15.xj, ...), custom_call_target="tpu_custom_call" | custom-call | tf_op jit(solution)/shard_map/update/pallas_call | solution.py:472
Async XLA Ops:
  0.0 1.0 %copy-start = (f32[512,256]{1,0:T(8,128)S(1)}, f32[512,256]{1,0:T(8,128)}, u32[]{:S(2)}) copy-start(f32[512,256]{1,0:T(8,128)} %a_ref.3) | copy-start | bytes 1572868
